TPU v7x, 128 devices: a whole 4x4x4 slice. The times are simulated.
128 devices in a mesh: dp: 8 (over x, core), mp: 16 (over y, z).
Axes of the slice: x: 4, y: 4, z: 4, core: 2. Of those that a mesh axis runs over, the one named last changes fastest.
Arguments:
- tokens: bfloat16 [512, 8192], P('dp', 'mp'), may hold values from -80 to 80
- frozen_gate_weight: bfloat16 [8192, 28672], P('mp', 'dp'), may hold values from -0.198873782 to 0.198873782
- frozen_up_weight: bfloat16 [8192, 28672], P('mp', 'dp'), may hold values from -0.198873782 to 0.198873782
- frozen_down_weight: bfloat16 [28672, 8192], P('dp', 'mp'), may hold values from -0.28347335 to 0.28347335
- gate_left_factor: bfloat16 [8192, 16], P('mp'), may hold values from -0.0625 to 0.0625
- gate_right_factor: bfloat16 [16, 28672], P(None, 'dp'), may hold values from -0.75 to 0.75
- up_left_factor: bfloat16 [8192, 16], P('mp'), may hold values from -0.0625 to 0.0625
- up_right_factor: bfloat16 [16, 28672], P(None, 'dp'), may hold values from -0.75 to 0.75
- down_left_factor: bfloat16 [28672, 16], P('dp'), may hold values from -0.03125 to 0.03125
- down_right_factor: bfloat16 [16, 8192], P(None, 'mp'), may hold values from -0.75 to 0.75
- gate_column_magnitude: float32 [28672], P('dp'), may hold values from 0.5 to 2
- up_column_magnitude: float32 [28672], P('dp'), may hold values from 0.5 to 2
- down_column_magnitude: float32 [8192], P('mp'), may hold values from 0.5 to 2
- cotangent: bfloat16 [512, 8192], P('dp', 'mp'), may hold values from -80 to 80
Outputs:
- feedforward_output: bfloat16 [512, 8192], P('dp', 'mp')
- token_input_gradient: bfloat16 [512, 8192], P('dp', 'mp')
- gate_magnitude_gradient: float32 [28672], P('dp')
- up_magnitude_gradient: float32 [28672], P('dp')
- down_magnitude_gradient: float32 [8192], P('mp')
- gate_right_factor_gradient: float32 [16, 28672], P(None, 'dp')
- gate_left_factor_gradient: float32 [8192, 16], P('mp')
- up_right_factor_gradient: float32 [16, 28672], P(None, 'dp')
- up_left_factor_gradient: float32 [8192, 16], P('mp')
- down_right_factor_gradient: float32 [16, 8192], P(None, 'mp')
- down_left_factor_gradient: float32 [28672, 16], P('dp')
All inputs are finite; a program needn't handle non-finite values.
Results may differ from a plain program's by a relative error of at most 0.03.
Values may be sent and summed in bfloat16 or wider, within the bound.
A program may use at most 192 MiB of HBM per device.

v0:
```python
import jax
import jax.numpy as jnp
from jax import lax
from jax.sharding import Mesh
from jax.sharding import PartitionSpec as P

MP = ("mp_0", "mp_1")
epsilon = 1e-06


def copy_for_each(shard, axis):
    devices = lax.axis_size(axis)
    return lax.all_to_all(
        jnp.broadcast_to(shard[None], (devices, *shard.shape)), axis, 0, 0, tiled=True
    )


def over_copies(shard, axis):
    return copy_for_each(shard, axis).sum(axis=0)


def packed_total(arrays, axis):
    ends = [0]
    for a in arrays:
        ends.append(ends[-1] + a.size)
    subtotal = over_copies(jnp.concatenate([a.ravel() for a in arrays]), axis)
    return tuple((subtotal[b:e].reshape(a.shape) for a, b, e in zip(arrays, ends, ends[1:])))


def joined_along(tiles, dim):
    dims = list(tiles.shape[1:])
    dims[dim] *= tiles.shape[0]
    return jnp.moveaxis(tiles, 0, dim).reshape(dims)


def collect(shard, axis, dim):
    tiles = copy_for_each(shard, axis)
    return joined_along(tiles, dim)


def taken_together(shard, axis):
    everything = copy_for_each(shard, axis)
    return jnp.sum(everything.astype(jnp.float32), axis=0)


def own_rows(terms, axes):
    subtotal = terms.astype(jnp.bfloat16)
    for axis in axes:
        subtotal = lax.psum_scatter(subtotal, axis, scatter_dimension=0, tiled=True)
    return subtotal.astype(jnp.float32)


def cut_along(shard, dim, devices):
    before, after = (shard.shape[:dim], shard.shape[dim + 1 :])
    return jnp.moveaxis(shard.reshape(*before, devices, -1, *after), dim, 0)


def sent_and_summed(shard, axis, dim):
    tiles = cut_along(shard, dim, lax.axis_size(axis))
    arrived = lax.all_to_all(tiles, axis, split_axis=0, concat_axis=0, tiled=True)
    return arrived.astype(jnp.float32).sum(axis=0)


def side_by_side(arrays, axis, dim, along):
    widths = [a.shape[along] for a in arrays]
    both = jnp.concatenate(arrays, axis=along)
    whole = lax.all_gather(both, axis, axis=dim, tiled=True)
    return tuple(jnp.split(whole, [sum(widths[:k]) for k in range(1, len(widths))], axis=along))


def matrix_product(left_side, right_side):
    return jnp.dot(left_side, right_side, preferred_element_type=jnp.float32)


def matrix_product_right_transposed(left_side, right_side):
    return lax.dot_general(
        left_side, right_side, (((1,), (1,)), ((), ())), preferred_element_type=jnp.float32
    )


def matrix_product_left_transposed(left_side, right_side):
    return lax.dot_general(
        left_side, right_side, (((0,), (0,)), ((), ())), preferred_element_type=jnp.float32
    )


def combine_adapter_columns(weight_matrix, left_factor, right_factor):
    combined_weight = weight_matrix.astype(jnp.float32) + matrix_product(left_factor, right_factor)
    return (
        combined_weight.astype(jnp.bfloat16),
        jnp.sum(combined_weight * combined_weight, axis=0),
    )


def activate(pre_pair, scale_gate, scale_up):
    width = scale_gate.shape[0]
    pre_gate = pre_pair[:, :width]
    pre_up = pre_pair[:, width:]
    gate_act = pre_gate * scale_gate
    up_act = pre_up * scale_up
    sigmoid_gate = jax.nn.sigmoid(gate_act)
    silu_gate = gate_act * sigmoid_gate
    hidden_state = (silu_gate * up_act).astype(jnp.bfloat16)
    return (hidden_state, (pre_gate, pre_up, gate_act, up_act, sigmoid_gate, silu_gate))


def gate_backward(grad_hidden, saved, scale_gate, scale_up):
    pre_gate, pre_up, gate_act, up_act, sigmoid_gate, silu_gate = saved
    grad_gate = grad_hidden * up_act * sigmoid_gate * (1.0 + gate_act * (1.0 - sigmoid_gate))
    grad_up = grad_hidden * silu_gate
    gate_logits = (grad_gate * scale_gate).astype(jnp.bfloat16)
    up_logits = (grad_up * scale_up).astype(jnp.bfloat16)
    return (
        gate_logits,
        up_logits,
        jnp.sum(grad_gate * pre_gate, axis=0),
        jnp.sum(grad_up * pre_up, axis=0),
    )


def per_device(
    tokens,
    frozen_gate_weight,
    frozen_up_weight,
    frozen_down_weight,
    gate_left_factor,
    gate_right_factor,
    up_left_factor,
    up_right_factor,
    down_left_factor,
    down_right_factor,
    gate_column_magnitude,
    up_column_magnitude,
    down_column_magnitude,
    cotangent,
):
    combined_gate_weight, gate_squared_columns = combine_adapter_columns(
        frozen_gate_weight, gate_left_factor, gate_right_factor
    )
    combined_up_weight, up_squared_columns = combine_adapter_columns(
        frozen_up_weight, up_left_factor, up_right_factor
    )
    combined_down_weight, down_squared_columns = combine_adapter_columns(
        frozen_down_weight, down_left_factor, down_right_factor
    )
    gate_squared_columns, up_squared_columns = packed_total(
        (gate_squared_columns, up_squared_columns), MP
    )
    down_squared_columns = over_copies(down_squared_columns, "dp")
    gate_column_norm = jnp.sqrt(gate_squared_columns + epsilon)
    up_column_norm = jnp.sqrt(up_squared_columns + epsilon)
    down_column_norm = jnp.sqrt(down_squared_columns + epsilon)
    scale_gate = gate_column_magnitude / gate_column_norm
    scale_up = up_column_magnitude / up_column_norm
    scale_down = down_column_magnitude / down_column_norm
    collected_rows = collect(tokens, "dp", 0)
    local_rows = collected_rows.shape[0] // lax.axis_size(MP)
    row_start = lax.axis_index(MP) * local_rows
    gate_projection_output, up_projection_output = (
        taken_together(
            matrix_product(collected_rows, gate_left_factor).astype(jnp.bfloat16), MP
        ).astype(jnp.float32),
        taken_together(
            matrix_product(collected_rows, up_left_factor).astype(jnp.bfloat16), MP
        ).astype(jnp.float32),
    )
    gate_projection_output = gate_projection_output.astype(jnp.bfloat16)
    up_projection_output = up_projection_output.astype(jnp.bfloat16)
    row_block = collected_rows
    pre_pair = own_rows(
        jnp.concatenate(
            [
                matrix_product(row_block, combined_gate_weight),
                matrix_product(row_block, combined_up_weight),
            ],
            axis=1,
        ),
        MP,
    )
    hidden_local, saved = activate(pre_pair, scale_gate, scale_up)
    hidden_state_full = lax.all_gather(hidden_local, MP, axis=0, tiled=True)
    row_block = hidden_state_full
    down_preactivation = sent_and_summed(
        matrix_product(row_block, combined_down_weight).astype(jnp.bfloat16), "dp", 0
    )
    feedforward_output = (down_preactivation * scale_down).astype(jnp.bfloat16)
    output_cotangent = cotangent.astype(jnp.float32)
    down_logits = (output_cotangent * scale_down).astype(jnp.bfloat16)
    down_projection_output, mag_down_sum = (
        taken_together(
            matrix_product(hidden_state_full, down_left_factor).astype(jnp.bfloat16), "dp"
        ).astype(jnp.float32),
        taken_together(
            jnp.sum(output_cotangent * down_preactivation, axis=0).astype(jnp.bfloat16), "dp"
        ).astype(jnp.float32),
    )
    down_projection_output = down_projection_output.astype(jnp.bfloat16)
    down_magnitude_gradient = mag_down_sum / down_column_norm
    down_logits_full = collect(down_logits, "dp", 0)
    down_backward_rows = (
        taken_together(
            matrix_product_right_transposed(down_logits_full, down_right_factor).astype(
                jnp.bfloat16
            ),
            MP,
        )
        .astype(jnp.float32)
        .astype(jnp.bfloat16)
    )
    down_right_factor_gradient = matrix_product_left_transposed(
        down_projection_output, down_logits_full
    )
    down_left_factor_gradient = matrix_product_left_transposed(
        hidden_state_full, down_backward_rows
    )
    row_block = down_logits_full
    grad_hidden = sent_and_summed(
        matrix_product_right_transposed(row_block, combined_down_weight).astype(jnp.bfloat16), MP, 0
    )
    gate_logits, up_logits, mag_gate_terms, mag_up_terms = gate_backward(
        grad_hidden, saved, scale_gate, scale_up
    )
    proj_gate_rows = lax.dynamic_slice_in_dim(gate_projection_output, row_start, local_rows, 0)
    proj_up_rows = lax.dynamic_slice_in_dim(up_projection_output, row_start, local_rows, 0)
    gate_backward_rows, up_backward_rows = packed_total(
        (
            matrix_product_right_transposed(gate_logits, gate_right_factor),
            matrix_product_right_transposed(up_logits, up_right_factor),
        ),
        "dp",
    )
    gate_backward_rows, up_backward_rows = side_by_side(
        (gate_backward_rows.astype(jnp.bfloat16), up_backward_rows.astype(jnp.bfloat16)), MP, 0, 1
    )
    (
        gate_magnitude_total,
        up_magnitude_total,
        gate_right_factor_gradient,
        up_right_factor_gradient,
    ) = (
        lax.psum(mag_gate_terms.astype(jnp.bfloat16), MP).astype(jnp.float32),
        lax.psum(mag_up_terms.astype(jnp.bfloat16), MP).astype(jnp.float32),
        lax.psum(
            matrix_product_left_transposed(proj_gate_rows, gate_logits).astype(jnp.bfloat16), MP
        ).astype(jnp.float32),
        lax.psum(
            matrix_product_left_transposed(proj_up_rows, up_logits).astype(jnp.bfloat16), MP
        ).astype(jnp.float32),
    )
    z_gate_full, z_up_full = side_by_side((gate_logits, up_logits), MP, 0, 1)
    gate_magnitude_gradient = gate_magnitude_total / gate_column_norm
    up_magnitude_gradient = up_magnitude_total / up_column_norm
    gate_left_factor_gradient = matrix_product_left_transposed(collected_rows, gate_backward_rows)
    up_left_factor_gradient = matrix_product_left_transposed(collected_rows, up_backward_rows)
    token_input_gradient = sent_and_summed(
        (
            matrix_product_right_transposed(z_gate_full, combined_gate_weight)
            + matrix_product_right_transposed(z_up_full, combined_up_weight)
        ).astype(jnp.bfloat16),
        "dp",
        0,
    ).astype(jnp.bfloat16)
    return (
        feedforward_output,
        token_input_gradient,
        gate_magnitude_gradient,
        up_magnitude_gradient,
        down_magnitude_gradient,
        gate_right_factor_gradient,
        gate_left_factor_gradient,
        up_right_factor_gradient,
        up_left_factor_gradient,
        down_right_factor_gradient,
        down_left_factor_gradient,
    )


def solution(mesh):
    torus = Mesh(mesh.devices.reshape(mesh.shape["dp"], 4, 4), ("dp", "mp_0", "mp_1"))
    in_specs = (
        P("dp", MP),
        P(MP, "dp"),
        P(MP, "dp"),
        P("dp", MP),
        P(MP, None),
        P(None, "dp"),
        P(MP, None),
        P(None, "dp"),
        P("dp", None),
        P(None, MP),
        P("dp"),
        P("dp"),
        P(MP),
        P("dp", MP),
    )
    out_specs = (
        P("dp", MP),
        P("dp", MP),
        P("dp"),
        P("dp"),
        P(MP),
        P(None, "dp"),
        P(MP, None),
        P(None, "dp"),
        P(MP, None),
        P(None, MP),
        P("dp", None),
    )
    return jax.shard_map(
        per_device, mesh=torus, in_specs=in_specs, out_specs=out_specs, check_vma=False
    )
```

profile of v0, /device:TPU:1, one launch (start us, length us, event | category | flops | bytes accessed | tf_op | source)
XLA Modules:
  0.0 435.9 jit_solution(9995394842297708845)
XLA Ops:
  7.2 1.7 broadcast_in_dim.20
  8.9 5.8 %all-to-all-start = ((bf16[8,64,512]{2,1,0:T(8,128)(2,1)}), bf16[8,64,512]{2,1,0:T(8,128)(2,1)S(1)}, u32[]{:S(2)}, u32[]{:S(2)}) async-start(bf16[8,64,512]{2,1,0:T(8,128)(2,1)} %broadcast_in_dim.20), calls=%async_computation | async-start | bytes 1048576 | tf_op jit(solution)/shard_map/all_to_all | solution.py:13
  14.8 5.3 %multiply_reduce_fusion.2 = (f32[3584]{0:T(1024)S(1)}, bf16[512,3584]{1,0:T(8,128)(2,1)}) fusion(bf16[512,16]{0,1:T(8,128)(2,1)} %param.18, bf16[16,3584]{1,0:T(8,128)(2,1)} %param.19, bf16[512,3584]{1,0:T(8,128)(2,1)} %param.15), kind=kOutput, calls=%fused_computation.5 | convolution fusion | flops 67891712 | bytes 7485440 | tf_op jit(solution)/shard_map/dot_general | solution.py:72
  20.1 3.2 multiply_reduce_fusion.1
  23.3 0.9 all-to-all-done
  24.2 4.3 fusion
  28.5 3.9 fusion.1
  32.4 5.5 %pad_maximum_fusion = bf16[512,7168]{0,1:T(8,128)(2,1)} fusion(bf16[512,3584]{0,1:T(8,128)(2,1)} %fusion.1, bf16[512,3584]{0,1:T(8,128)(2,1)S(1)} %fusion), kind=kLoop, calls=%fused_computation | loop fusion | flops 14680064 | bytes 14680064 | tf_op jit(solution)/shard_map/concatenate | solution.py:171
  38.0 10.0 %copy.52 = bf16[512,7168]{1,0:T(8,128)(2,1)} copy(bf16[512,7168]{0,1:T(8,128)(2,1)} %pad_maximum_fusion) | data formatting | bytes 14680064
  48.0 0.7 copy-done.6
  48.7 5.2 %multiply_reduce_fusion = (f32[512]{0:T(512)S(1)}, bf16[3584,512]{1,0:T(8,128)(2,1)}) fusion(bf16[3584,16]{0,1:T(8,128)(2,1)S(1)} %copy-done, bf16[16,512]{1,0:T(8,128)(2,1)S(1)} %copy-done.6, bf16[3584,512]{1,0:T(8,128)(2,1)} %param.17), kind=kOutput, calls=%fused_computation.2 | convolution fusion | flops 67894784 | bytes 7473152 | tf_op jit(solution)/shard_map/dot_general | solution.py:72
  53.9 8.4 %all_to_all.69 = f32[8,1,512]{2,1,0:T(1,128)S(1)} all-to-all(f32[8,1,512]{2,1,0:T(1,128)S(1)} %broadcast_in_dim.22), channel_id=1, replica_groups=mesh['dp'=8,'mp_0'=4,'mp_1'=4] {'dp'}, dimensions={0} | all-to-all | bytes 32768 | tf_op jit(solution)/shard_map/all_to_all | solution.py:13
  62.4 0.9 broadcast_in_dim.23
  63.3 4.0 all-to-all-start.4
  67.3 9.5 %all-to-all-done.4 = bf16[8,64,512]{2,1,0:T(8,128)(2,1)S(1)} async-done(((bf16[8,64,512]{2,1,0:T(8,128)(2,1)}), bf16[8,64,512]{2,1,0:T(8,128)(2,1)S(1)}, u32[]{:S(2)}, u32[]{:S(2)}) %all-to-all-start.4) | async-done | bytes 524320 | tf_op jit(solution)/shard_map/all_to_all | solution.py:13
  76.8 1.0 broadcast_in_dim.21
  77.8 7.8 %all-to-all-start.1 = ((f32[16,1,7168]{2,1,0:T(1,128)}), f32[16,1,7168]{2,1,0:T(1,128)S(1)}, u32[]{:S(2)}, u32[]{:S(2)}) async-start(f32[16,1,7168]{2,1,0:T(1,128)} %broadcast_in_dim.21), calls=%async_computation.1 | async-start | bytes 917504 | tf_op jit(solution)/shard_map/all_to_all | solution.py:13
  85.6 6.1 %convolution_convert_fusion = bf16[512,3584]{1,0:T(8,128)(2,1)} fusion(bf16[512,512]{1,0:T(8,128)(2,1)S(1)} %bitcast.57, bf16[3584,512]{1,0:T(8,128)(2,1)} %get-tuple-element.29), kind=kOutput, calls=%fused_computation.8 | convolution fusion | flops 1880883200 | bytes 7864320 | tf_op jit(solution)/shard_map/dot_general | solution.py:76
  91.7 7.4 %all-to-all-done.1 = f32[16,1,7168]{2,1,0:T(1,128)S(1)} async-done(((f32[16,1,7168]{2,1,0:T(1,128)}), f32[16,1,7168]{2,1,0:T(1,128)S(1)}, u32[]{:S(2)}, u32[]{:S(2)}) %all-to-all-start.1) | async-done | bytes 458784 | tf_op jit(solution)/shard_map/all_to_all | solution.py:13
  99.0 6.0 %all-to-all-start.5 = ((bf16[16,32,3584]{2,1,0:T(8,128)(2,1)}), bf16[16,32,3584]{2,1,0:T(8,128)(2,1)}, u32[]{:S(2)}, u32[]{:S(2)}) async-start(bf16[16,32,3584]{2,1,0:T(8,128)(2,1)} %bitcast.60), calls=%async_computation.5 | async-start | bytes 7340032 | tf_op jit(solution)/shard_map/all_to_all | solution.py:60
  105.1 55.5 %reduce-scatter.7.cloned.1.call-done = bf16[128,7168]{1,0:T(8,128)(2,1)} async-done(((bf16[512,7168]{1,0:T(8,128)(2,1)}), bf16[128,7168]{1,0:T(8,128)(2,1)}) %reduce-scatter.7.cloned.1.call-update) | async-done | bytes 1835024
  161.0 6.8 %all-to-all-done.5 = bf16[16,32,3584]{2,1,0:T(8,128)(2,1)} async-done(((bf16[16,32,3584]{2,1,0:T(8,128)(2,1)}), bf16[16,32,3584]{2,1,0:T(8,128)(2,1)}, u32[]{:S(2)}, u32[]{:S(2)}) %all-to-all-start.5) | async-done | bytes 3670048 | tf_op jit(solution)/shard_map/all_to_all | solution.py:60
  167.8 2.6 convert_reduce_fusion
  170.4 24.2 %reduce-scatter.9.cloned.1.call-done = bf16[32,7168]{1,0:T(8,128)(2,1)} async-done(((bf16[128,7168]{1,0:T(8,128)(2,1)}), bf16[32,7168]{1,0:T(8,128)(2,1)}) %reduce-scatter.9.cloned.1.call-update) | async-done | bytes 458768 | tf_op jit(solution)/shard_map/reduce_scatter | solution.py:49
  194.6 1.1 convert_element_type.124
  195.7 1.0 multiply_reduce_fusion.3
  197.0 0.7 broadcast_in_dim.25
  197.8 5.0 %all-to-all-start.8 = ((bf16[16,512,16]{1,2,0:T(8,128)(2,1)}), bf16[16,512,16]{1,2,0:T(8,128)(2,1)S(1)}, u32[]{:S(2)}, u32[]{:S(2)}) async-start(bf16[16,512,16]{1,2,0:T(8,128)(2,1)} %broadcast_in_dim.25), calls=%async_computation.8 | async-start | bytes 524288 | tf_op jit(solution)/shard_map/all_to_all | solution.py:13
  203.0 7.2 %all-to-all-done.8 = bf16[16,512,16]{1,2,0:T(8,128)(2,1)S(1)} async-done(((bf16[16,512,16]{1,2,0:T(8,128)(2,1)}), bf16[16,512,16]{1,2,0:T(8,128)(2,1)S(1)}, u32[]{:S(2)}, u32[]{:S(2)}) %all-to-all-start.8) | async-done | bytes 262176 | tf_op jit(solution)/shard_map/all_to_all | solution.py:13
  210.3 0.7 broadcast_in_dim.27
  211.0 3.5 all-to-all-start.10
  214.6 7.5 %all-to-all-done.10 = bf16[16,512,16]{1,2,0:T(8,128)(2,1)S(1)} async-done(((bf16[16,512,16]{1,2,0:T(8,128)(2,1)}), bf16[16,512,16]{1,2,0:T(8,128)(2,1)S(1)}, u32[]{:S(2)}, u32[]{:S(2)}) %all-to-all-start.10) | async-done | bytes 262176 | tf_op jit(solution)/shard_map/all_to_all | solution.py:13
  222.2 0.9 convolution_convert_fusion.4
  223.1 0.9 convolution_convert_fusion.3
  224.1 0.8 pad_maximum_fusion.1
  225.2 12.9 %all_to_all.70 = bf16[16,512,16]{1,2,0:T(8,128)(2,1)S(1)} all-to-all(bf16[16,512,16]{1,2,0:T(8,128)(2,1)S(1)} %broadcast_in_dim.29), channel_id=1, replica_groups=mesh['dp'=8,'mp_0'=4,'mp_1'=4] {'mp_0','mp_1'}, dimensions={0} | all-to-all | bytes 524288 | tf_op jit(solution)/shard_map/all_to_all | solution.py:13
  238.7 0.6 broadcast_in_dim.26
  239.4 8.5 %all-to-all-start.9 = ((f32[8,1,1024]{2,1,0:T(1,128)}), f32[8,1,1024]{2,1,0:T(1,128)S(1)}, u32[]{:S(2)}, u32[]{:S(2)}) async-start(f32[8,1,1024]{2,1,0:T(1,128)} %broadcast_in_dim.26), calls=%async_computation.9 | async-start | bytes 65536 | tf_op jit(solution)/shard_map/all_to_all | solution.py:13
  247.8 57.0 %all-reduce = (bf16[3584]{0:T(1024)(128)(2,1)S(1)}, bf16[3584]{0:T(1024)(128)(2,1)S(1)}) all-reduce(bf16[3584]{0:T(1024)(128)(2,1)S(1)} %get-tuple-element.12, bf16[3584]{0:T(1024)(128)(2,1)S(1)} %get-tuple-element.11), channel_id=1, replica_groups=mesh['dp'=8,'mp_0'=4,'mp_1'=4] {'mp_0','mp_1'}, use_global_device_ids=true, to_apply=%region_11.0 | all-reduce | flops 7168 | bytes 28672 | tf_op jit(solution)/shard_map/psum | solution.py:241
  304.9 0.6 convert_divide_fusion
  305.8 15.6 %all_gather.11 = bf16[512,32]{1,0:T(8,128)(2,1)S(1)} all-gather(bf16[32,32]{1,0:T(8,128)(2,1)S(1)} %pad_maximum_fusion.3), channel_id=1, replica_groups=mesh['dp'=8,'mp_0'=4,'mp_1'=4] {'mp_0','mp_1'}, dimensions={0}, use_global_device_ids=true | all-gather | bytes 34816 | tf_op jit(solution)/shard_map/all_gather | solution.py:67
  321.4 0.9 convolution_bitcast_fusion
  322.3 3.1 convolution_convert_fusion.5
  325.4 0.7 broadcast_in_dim.28
  326.1 23.8 %all-to-all-start.11 = ((bf16[8,512,16]{1,2,0:T(8,128)(2,1)}), bf16[8,512,16]{1,2,0:T(8,128)(2,1)S(1)}, u32[]{:S(2)}, u32[]{:S(2)}) async-start(bf16[8,512,16]{1,2,0:T(8,128)(2,1)} %broadcast_in_dim.28), calls=%async_computation.11 | async-start | bytes 262144 | tf_op jit(solution)/shard_map/all_to_all | solution.py:13
  349.9 6.0 %fusion.23 = bf16[512,512]{1,0:T(8,128)(2,1)} fusion(bf16[512,3584]{1,0:T(8,128)(2,1)} %all-gather.3.cloned.1.call-done, bf16[3584,512]{1,0:T(8,128)(2,1)} %get-tuple-element.29), kind=kOutput, calls=%fused_computation.28 | convolution fusion | flops 1879310336 | bytes 7864320 | tf_op jit(solution)/shard_map/dot_general | solution.py:72
  355.9 4.8 %all-to-all-start.2 = ((bf16[8,64,512]{2,1,0:T(8,128)(2,1)}), bf16[8,64,512]{2,1,0:T(8,128)(2,1)S(1)}, u32[]{:S(2)}, u32[]{:S(2)}) async-start(bf16[8,64,512]{2,1,0:T(8,128)(2,1)} %bitcast.3), calls=%async_computation.2 | async-start | bytes 1048576 | tf_op jit(solution)/shard_map/all_to_all | solution.py:60
  360.7 0.8 convolution_bitcast_fusion.1
  361.5 1.6 convert_element_type.146
  363.1 1.6 convert_element_type.151
  364.7 3.3 fusion.45
  368.1 2.1 all-to-all-done.2
  370.3 0.7 fusion.28
  371.4 0.7 reduce.9
  372.1 0.6 reshape.111
  372.8 4.1 all-to-all-start.7
  376.9 28.2 %all-gather.5.cloned.1.call-done = bf16[512,7168]{1,0:T(8,128)(2,1)} async-done(((bf16[32,7168]{1,0:T(8,128)(2,1)}), bf16[512,7168]{1,0:T(8,128)(2,1)}) %all-gather.5.cloned.1.call-update) | async-done | bytes 7340048 | tf_op jit(solution)/shard_map/all_gather | solution.py:67
  405.1 5.4 %fusion.2 = f32[512,512]{1,0:T(8,128)S(1)} fusion(bf16[512,7168]{1,0:T(8,128)(2,1)} %all-gather.5.cloned.1.call-done, bf16[512,3584]{1,0:T(8,128)(2,1)} %get-tuple-element.31), kind=kOutput, calls=%fused_computation.15 | convolution fusion | flops 1879048192 | bytes 8388608 | tf_op jit(solution)/shard_map/dot_general | solution.py:76
  410.5 0.9 copy-done.12
  411.4 2.9 fusion.18
  414.2 4.9 %all-to-all-start.6 = ((bf16[8,64,512]{2,1,0:T(8,128)(2,1)}), bf16[8,64,512]{2,1,0:T(8,128)(2,1)S(1)}, u32[]{:S(2)}, u32[]{:S(2)}) async-start(bf16[8,64,512]{2,1,0:T(8,128)(2,1)} %bitcast.6), calls=%async_computation.6 | async-start | bytes 1048576 | tf_op jit(solution)/shard_map/all_to_all | solution.py:60
  419.2 0.8 fusion.44
  420.6 8.1 %all-to-all-done.6 = bf16[8,64,512]{2,1,0:T(8,128)(2,1)S(1)} async-done(((bf16[8,64,512]{2,1,0:T(8,128)(2,1)}), bf16[8,64,512]{2,1,0:T(8,128)(2,1)S(1)}, u32[]{:S(2)}, u32[]{:S(2)}) %all-to-all-start.6) | async-done | bytes 524320 | tf_op jit(solution)/shard_map/all_to_all | solution.py:60
  428.6 0.7 reduce_sum.175
  (73 shorter events, 3.8 us)
Async XLA Ops:
  7.2 40.8 %copy-start = (bf16[3584,16]{0,1:T(8,128)(2,1)S(1)}, bf16[3584,16]{0,1:T(8,128)(2,1)}, u32[]{:S(2)}) copy-start(bf16[3584,16]{0,1:T(8,128)(2,1)} %param.22) | copy-start | bytes 344068
  8.9 15.3 %all-to-all-start = ((bf16[8,64,512]{2,1,0:T(8,128)(2,1)}), bf16[8,64,512]{2,1,0:T(8,128)(2,1)S(1)}, u32[]{:S(2)}, u32[]{:S(2)}) async-start(bf16[8,64,512]{2,1,0:T(8,128)(2,1)} %broadcast_in_dim.20), calls=%async_computation | async-start | bytes 1048576 | tf_op jit(solution)/shard_map/all_to_all | solution.py:13
  14.7 5.4 %copy-start.3 = (bf16[16,3584]{1,0:T(8,128)(2,1)S(1)}, bf16[16,3584]{1,0:T(8,128)(2,1)}, u32[]{:S(2)}) copy-start(bf16[16,3584]{1,0:T(8,128)(2,1)} %param.21) | copy-start | bytes 344068
  14.7 5.4 %copy-start.5 = (bf16[512,16]{0,1:T(8,128)(2,1)S(1)}, bf16[512,16]{0,1:T(8,128)(2,1)}, u32[]{:S(2)}) copy-start(bf16[512,16]{0,1:T(8,128)(2,1)} %param.20) | copy-start | bytes 49156
  14.7 145.9 %reduce-scatter.7.cloned.1.call-start = ((), (), s32[]{:S(2)}) async-start(), calls=%async_computation.17 | async-start | bytes 9175040
  14.7 5.4 %copy-start.11 = (bf16[512,3584]{1,0:T(8,128)(2,1)S(1)}, bf16[512,3584]{1,0:T(8,128)(2,1)}, u32[]{:S(2)}) copy-start(bf16[512,3584]{1,0:T(8,128)(2,1)} %param.16) | copy-start | bytes 11010052
  24.2 4.3 copy-start.13
  47.9 0.7 copy-start.6
  48.7 13.7 %copy-start.9 = (f32[512]{0:T(512)S(1)}, f32[512]{0:T(512)}, u32[]{:S(2)}) copy-start(f32[512]{0:T(512)} %param.26) | copy-start | bytes 6148
  48.7 13.7 %copy-start.1 = (bf16[64,512]{1,0:T(8,128)(2,1)S(1)}, bf16[64,512]{1,0:T(8,128)(2,1)}, u32[]{:S(2)}) copy-start(bf16[64,512]{1,0:T(8,128)(2,1)} %param.27) | copy-start | bytes 196612
  63.3 13.5 %all-to-all-start.4 = ((bf16[8,64,512]{2,1,0:T(8,128)(2,1)}), bf16[8,64,512]{2,1,0:T(8,128)(2,1)S(1)}, u32[]{:S(2)}, u32[]{:S(2)}) async-start(bf16[8,64,512]{2,1,0:T(8,128)(2,1)} %broadcast_in_dim.23), calls=%async_computation.4 | async-start | bytes 1048576 | tf_op jit(solution)/shard_map/all_to_all | solution.py:13
  77.8 21.2 %all-to-all-start.1 = ((f32[16,1,7168]{2,1,0:T(1,128)}), f32[16,1,7168]{2,1,0:T(1,128)S(1)}, u32[]{:S(2)}, u32[]{:S(2)}) async-start(f32[16,1,7168]{2,1,0:T(1,128)} %broadcast_in_dim.21), calls=%async_computation.1 | async-start | bytes 917504 | tf_op jit(solution)/shard_map/all_to_all | solution.py:13
  99.0 61.9 %copy-start.7 = (f32[3584]{0:T(1024)S(1)}, f32[3584]{0:T(1024)}, u32[]{:S(2)}) copy-start(f32[3584]{0:T(1024)} %param.24) | copy-start | bytes 43012
  99.0 61.9 %copy-start.8 = (f32[3584]{0:T(1024)S(1)}, f32[3584]{0:T(1024)}, u32[]{:S(2)}) copy-start(f32[3584]{0:T(1024)} %param.25) | copy-start | bytes 43012
  99.0 68.8 %all-to-all-start.5 = ((bf16[16,32,3584]{2,1,0:T(8,128)(2,1)}), bf16[16,32,3584]{2,1,0:T(8,128)(2,1)}, u32[]{:S(2)}, u32[]{:S(2)}) async-start(bf16[16,32,3584]{2,1,0:T(8,128)(2,1)} %bitcast.60), calls=%async_computation.5 | async-start | bytes 7340032 | tf_op jit(solution)/shard_map/all_to_all | solution.py:60
  105.0 89.6 %reduce-scatter.9.cloned.1.call-start = ((), (), s32[]{:S(2)}) async-start(), calls=%async_computation.18 | async-start | bytes 2293760 | tf_op jit(solution)/shard_map/reduce_scatter | solution.py:49
  160.6 161.7 %all-gather.3.cloned.1.call-start = ((), (), s32[]{:S(2)}) async-start(), calls=%async_computation.15 | async-start | bytes 3899392 | tf_op jit(solution)/shard_map/all_gather | solution.py:181
  161.0 35.8 %copy-start.4 = (bf16[512,16]{0,1:T(8,128)(2,1)S(1)}, bf16[512,16]{0,1:T(8,128)(2,1)}, u32[]{:S(2)}) copy-start(bf16[512,16]{0,1:T(8,128)(2,1)} %param.18) | copy-start | bytes 49156
  197.0 41.1 %copy-start.2 = (bf16[16,3584]{1,0:T(8,128)(2,1)S(1)}, bf16[16,3584]{1,0:T(8,128)(2,1)}, u32[]{:S(2)}) copy-start(bf16[16,3584]{1,0:T(8,128)(2,1)} %param.19) | copy-start | bytes 344068
  197.8 12.5 %all-to-all-start.8 = ((bf16[16,512,16]{1,2,0:T(8,128)(2,1)}), bf16[16,512,16]{1,2,0:T(8,128)(2,1)S(1)}, u32[]{:S(2)}, u32[]{:S(2)}) async-start(bf16[16,512,16]{1,2,0:T(8,128)(2,1)} %broadcast_in_dim.25), calls=%async_computation.8 | async-start | bytes 524288 | tf_op jit(solution)/shard_map/all_to_all | solution.py:13
  211.0 11.2 %all-to-all-start.10 = ((bf16[16,512,16]{1,2,0:T(8,128)(2,1)}), bf16[16,512,16]{1,2,0:T(8,128)(2,1)S(1)}, u32[]{:S(2)}, u32[]{:S(2)}) async-start(bf16[16,512,16]{1,2,0:T(8,128)(2,1)} %broadcast_in_dim.27), calls=%async_computation.10 | async-start | bytes 524288 | tf_op jit(solution)/shard_map/all_to_all | solution.py:13
  214.5 147.0 %all-reduce.4.cloned.1.call-start = ((), (), s32[]{:S(2)}) async-start(), calls=%async_computation.19 | async-start | bytes 458752 | tf_op jit(solution)/shard_map/psum | solution.py:243
  224.0 181.1 %all-gather.5.cloned.1.call-start = ((), (), s32[]{:S(2)}) async-start(), calls=%async_computation.16 | async-start | bytes 7798784 | tf_op jit(solution)/shard_map/all_gather | solution.py:67
  239.4 66.1 %all-to-all-start.9 = ((f32[8,1,1024]{2,1,0:T(1,128)}), f32[8,1,1024]{2,1,0:T(1,128)S(1)}, u32[]{:S(2)}, u32[]{:S(2)}) async-start(f32[8,1,1024]{2,1,0:T(1,128)} %broadcast_in_dim.26), calls=%async_computation.9 | async-start | bytes 65536 | tf_op jit(solution)/shard_map/all_to_all | solution.py:13
  326.1 29.8 %all-to-all-start.11 = ((bf16[8,512,16]{1,2,0:T(8,128)(2,1)}), bf16[8,512,16]{1,2,0:T(8,128)(2,1)S(1)}, u32[]{:S(2)}, u32[]{:S(2)}) async-start(bf16[8,512,16]{1,2,0:T(8,128)(2,1)} %broadcast_in_dim.28), calls=%async_computation.11 | async-start | bytes 262144 | tf_op jit(solution)/shard_map/all_to_all | solution.py:13
  355.9 14.3 %all-to-all-start.2 = ((bf16[8,64,512]{2,1,0:T(8,128)(2,1)}), bf16[8,64,512]{2,1,0:T(8,128)(2,1)S(1)}, u32[]{:S(2)}, u32[]{:S(2)}) async-start(bf16[8,64,512]{2,1,0:T(8,128)(2,1)} %bitcast.3), calls=%async_computation.2 | async-start | bytes 1048576 | tf_op jit(solution)/shard_map/all_to_all | solution.py:60
  372.8 41.5 %all-to-all-start.7 = ((bf16[8,2,256]{2,1,0:T(2,128)(2,1)}), bf16[8,2,256]{2,1,0:T(2,128)(2,1)S(1)}, u32[]{:S(2)}, u32[]{:S(2)}) async-start(bf16[8,2,256]{2,1,0:T(2,128)(2,1)} %reshape.111), calls=%async_computation.7 | async-start | bytes 16384 | tf_op jit(solution)/shard_map/all_to_all | solution.py:13
  405.1 5.4 %copy-start.10 = (bf16[512,7168]{1,0:T(8,128)(2,1)S(1)}, bf16[512,7168]{1,0:T(8,128)(2,1)}, u32[]{:S(2)}) copy-start(bf16[512,7168]{1,0:T(8,128)(2,1)} %all-gather.5.cloned.1.call-done) | copy-start | bytes 22020100
  405.1 6.3 %copy-start.12 = (bf16[512,3584]{1,0:T(8,128)(2,1)S(1)}, bf16[512,3584]{1,0:T(8,128)(2,1)}, u32[]{:S(2)}) copy-start(bf16[512,3584]{1,0:T(8,128)(2,1)} %get-tuple-element.33) | copy-start | bytes 11010052
  414.2 14.4 %all-to-all-start.6 = ((bf16[8,64,512]{2,1,0:T(8,128)(2,1)}), bf16[8,64,512]{2,1,0:T(8,128)(2,1)S(1)}, u32[]{:S(2)}, u32[]{:S(2)}) async-start(bf16[8,64,512]{2,1,0:T(8,128)(2,1)} %bitcast.6), calls=%async_computation.6 | async-start | bytes 1048576 | tf_op jit(solution)/shard_map/all_to_all | solution.py:60
Sparse Core Ops, SparseCore 0:
  48.1 112.4 reduce-scatter.6
  163.0 31.6 reduce-scatter.8
  197.4 52.6 all-gather.2
  253.9 82.0 all-reduce.3
  338.3 66.7 all-gather.4
where the time goes:
time: 438 us; the launch traced here: 436 us
  waiting for transfers between devices  158 us (36%)
  blocking collectives  93.9 us (21%)
  starting transfers between devices  78.5 us (18%)
  matrix products  54.1 us (12%)
  local copies, waits for them, and re-layouts  19.5 us (4%)
  other arithmetic  18.4 us (4%)
  between operations  14 us (3%)
    all_to_all x8, starting transfers between devices, copy_for_each(): lax.all_to_all(jnp.broadcast_to(shard[None], (devices, *shard.shape)), ax...  62.6 us
    psum x1, blocking collectives, per_device(): lax.psum(mag_gate_terms.astype(jnp.bfloat16), MP).astype(jnp.float32)  57 us
    unnamed x6, waiting for transfers between devices  55.6 us
    all_to_all x8, waiting for transfers between devices, copy_for_each(): lax.all_to_all(jnp.broadcast_to(shard[None], (devices, *shard.shape)), ax...  32.5 us
    dot_general x9, matrix products, matrix_product(): return jnp.dot(left_side, right_side, preferred_element_type=jnp.float32)  31.6 us
    all_gather x1, waiting for transfers between devices, side_by_side(): whole = lax.all_gather(both, axis, axis=dim, tiled=True)  28.2 us
    reduce_scatter x1, waiting for transfers between devices, own_rows(): subtotal = lax.psum_scatter(subtotal, axis, scatter_dimension=0, tiled=True)  24.2 us
    all_to_all x2, blocking collectives, copy_for_each(): lax.all_to_all(jnp.broadcast_to(shard[None], (devices, *shard.shape)), ax...  21.3 us
  transfers between devices with their start and end apart: 16, of which 11 were waited for; matrix products, arithmetic and copies ran while one was open for 14% of the time, Pallas kernels for 0%

commit v1 on v0

--- a/solution.py
+++ b/solution.py
@@ -232,13 +232,19 @@
     gate_backward_rows, up_backward_rows = side_by_side(
         (gate_backward_rows.astype(jnp.bfloat16), up_backward_rows.astype(jnp.bfloat16)), MP, 0, 1
     )
+
+    def _balance_record(inputs, across, which_axis):
+        for nth in (across, which_axis):
+            inputs = lax.psum(inputs, axis_name=nth)
+        return inputs
+
     (
         gate_magnitude_total,
         up_magnitude_total,
         gate_right_factor_gradient,
         up_right_factor_gradient,
     ) = (
-        lax.psum(mag_gate_terms.astype(jnp.bfloat16), MP).astype(jnp.float32),
+        _balance_record(mag_gate_terms.astype(jnp.bfloat16), "mp_0", "mp_1").astype(jnp.float32),
         lax.psum(mag_up_terms.astype(jnp.bfloat16), MP).astype(jnp.float32),
         lax.psum(
             matrix_product_left_transposed(proj_gate_rows, gate_logits).astype(jnp.bfloat16), MP

time: 438 us -> 438 us (level)
  waiting for transfers between devices: 158 us -> 173 us
  blocking collectives: 93.9 us -> 83.4 us
  starting transfers between devices: 78.5 us -> 73.7 us
    all_gather x1, waiting for transfers between devices: 28.2 us -> 43.5 us  [side_by_side(): whole = lax.all_gather(both, axis, axis=dim, tiled=True)]
    psum x1 -> x3, blocking collectives: 57 us -> 44.4 us  [the longest x1 30.5 us: per_device(): lax.psum(mag_up_terms.astype(jnp.bfloat16), MP).astype(jnp.float32)]
    all_to_all x8, starting transfers between devices: 62.6 us -> 57.8 us  [copy_for_each(): lax.all_to_all(jnp.broadcast_to(shard[None], (devices, *shard.shape)), ax...]
where the time goes in v1:
time: 438 us; the launch traced here: 436 us
  waiting for transfers between devices  173 us (39%)
  blocking collectives  83.4 us (19%)
  starting transfers between devices  73.7 us (17%)
  matrix products  54.1 us (12%)
  local copies, waits for them, and re-layouts  19.5 us (4%)
  other arithmetic  18.4 us (4%)
  between operations  14.1 us (3%)
    all_to_all x8, starting transfers between devices, copy_for_each(): lax.all_to_all(jnp.broadcast_to(shard[None], (devices, *shard.shape)), ax...  57.8 us
    unnamed x6, waiting for transfers between devices  55.6 us
    all_gather x1, waiting for transfers between devices, side_by_side(): whole = lax.all_gather(both, axis, axis=dim, tiled=True)  43.5 us
    all_to_all x8, waiting for transfers between devices, copy_for_each(): lax.all_to_all(jnp.broadcast_to(shard[None], (devices, *shard.shape)), ax...  32.5 us
    dot_general x9, matrix products, matrix_product(): return jnp.dot(left_side, right_side, preferred_element_type=jnp.float32)  31.5 us
    psum x1, blocking collectives, per_device(): lax.psum(mag_up_terms.astype(jnp.bfloat16), MP).astype(jnp.float32)  30.5 us
    reduce_scatter x1, waiting for transfers between devices, own_rows(): subtotal = lax.psum_scatter(subtotal, axis, scatter_dimension=0, tiled=True)  24.2 us
    all_to_all x2, blocking collectives, copy_for_each(): lax.all_to_all(jnp.broadcast_to(shard[None], (devices, *shard.shape)), ax...  21.3 us
  transfers between devices with their start and end apart: 16, of which 11 were waited for; matrix products, arithmetic and copies ran while one was open for 14% of the time, Pallas kernels for 0%

profile of v1, /device:TPU:1, one launch (start us, length us, event | category | flops | bytes accessed | tf_op | source)
XLA Modules:
  0.0 435.9 jit_solution(3908132445313161355)
XLA Ops:
  7.2 1.7 broadcast_in_dim.20
  8.9 5.8 %all-to-all-start = ((bf16[8,64,512]{2,1,0:T(8,128)(2,1)}), bf16[8,64,512]{2,1,0:T(8,128)(2,1)S(1)}, u32[]{:S(2)}, u32[]{:S(2)}) async-start(bf16[8,64,512]{2,1,0:T(8,128)(2,1)} %broadcast_in_dim.20), calls=%async_computation | async-start | bytes 1048576 | tf_op jit(solution)/shard_map/all_to_all | solution.py:13
  14.8 5.3 %multiply_reduce_fusion.2 = (f32[3584]{0:T(1024)S(1)}, bf16[512,3584]{1,0:T(8,128)(2,1)}) fusion(bf16[512,16]{0,1:T(8,128)(2,1)} %param.18, bf16[16,3584]{1,0:T(8,128)(2,1)} %param.19, bf16[512,3584]{1,0:T(8,128)(2,1)} %param.15), kind=kOutput, calls=%fused_computation.5 | convolution fusion | flops 67891712 | bytes 7485440 | tf_op jit(solution)/shard_map/dot_general | solution.py:72
  20.1 3.2 multiply_reduce_fusion.1
  23.3 0.9 all-to-all-done
  24.2 4.3 fusion
  28.5 3.9 fusion.1
  32.4 5.5 %pad_maximum_fusion = bf16[512,7168]{0,1:T(8,128)(2,1)} fusion(bf16[512,3584]{0,1:T(8,128)(2,1)} %fusion.1, bf16[512,3584]{0,1:T(8,128)(2,1)S(1)} %fusion), kind=kLoop, calls=%fused_computation | loop fusion | flops 14680064 | bytes 14680064 | tf_op jit(solution)/shard_map/concatenate | solution.py:171
  38.0 10.0 %copy.52 = bf16[512,7168]{1,0:T(8,128)(2,1)} copy(bf16[512,7168]{0,1:T(8,128)(2,1)} %pad_maximum_fusion) | data formatting | bytes 14680064
  48.0 0.7 copy-done.6
  48.7 5.2 %multiply_reduce_fusion = (f32[512]{0:T(512)S(1)}, bf16[3584,512]{1,0:T(8,128)(2,1)}) fusion(bf16[3584,16]{0,1:T(8,128)(2,1)S(1)} %copy-done, bf16[16,512]{1,0:T(8,128)(2,1)S(1)} %copy-done.6, bf16[3584,512]{1,0:T(8,128)(2,1)} %param.17), kind=kOutput, calls=%fused_computation.2 | convolution fusion | flops 67894784 | bytes 7473152 | tf_op jit(solution)/shard_map/dot_general | solution.py:72
  53.9 8.4 %all_to_all.69 = f32[8,1,512]{2,1,0:T(1,128)S(1)} all-to-all(f32[8,1,512]{2,1,0:T(1,128)S(1)} %broadcast_in_dim.22), channel_id=1, replica_groups=mesh['dp'=8,'mp_0'=4,'mp_1'=4] {'dp'}, dimensions={0} | all-to-all | bytes 32768 | tf_op jit(solution)/shard_map/all_to_all | solution.py:13
  62.4 0.9 broadcast_in_dim.23
  63.3 4.0 all-to-all-start.4
  67.3 9.5 %all-to-all-done.4 = bf16[8,64,512]{2,1,0:T(8,128)(2,1)S(1)} async-done(((bf16[8,64,512]{2,1,0:T(8,128)(2,1)}), bf16[8,64,512]{2,1,0:T(8,128)(2,1)S(1)}, u32[]{:S(2)}, u32[]{:S(2)}) %all-to-all-start.4) | async-done | bytes 524320 | tf_op jit(solution)/shard_map/all_to_all | solution.py:13
  76.8 1.0 broadcast_in_dim.21
  77.8 7.8 %all-to-all-start.1 = ((f32[16,1,7168]{2,1,0:T(1,128)}), f32[16,1,7168]{2,1,0:T(1,128)S(1)}, u32[]{:S(2)}, u32[]{:S(2)}) async-start(f32[16,1,7168]{2,1,0:T(1,128)} %broadcast_in_dim.21), calls=%async_computation.1 | async-start | bytes 917504 | tf_op jit(solution)/shard_map/all_to_all | solution.py:13
  85.6 6.1 %convolution_convert_fusion = bf16[512,3584]{1,0:T(8,128)(2,1)} fusion(bf16[512,512]{1,0:T(8,128)(2,1)S(1)} %bitcast.57, bf16[3584,512]{1,0:T(8,128)(2,1)} %get-tuple-element.27), kind=kOutput, calls=%fused_computation.8 | convolution fusion | flops 1880883200 | bytes 7864320 | tf_op jit(solution)/shard_map/dot_general | solution.py:76
  91.7 7.4 %all-to-all-done.1 = f32[16,1,7168]{2,1,0:T(1,128)S(1)} async-done(((f32[16,1,7168]{2,1,0:T(1,128)}), f32[16,1,7168]{2,1,0:T(1,128)S(1)}, u32[]{:S(2)}, u32[]{:S(2)}) %all-to-all-start.1) | async-done | bytes 458784 | tf_op jit(solution)/shard_map/all_to_all | solution.py:13
  99.0 6.0 %all-to-all-start.5 = ((bf16[16,32,3584]{2,1,0:T(8,128)(2,1)}), bf16[16,32,3584]{2,1,0:T(8,128)(2,1)}, u32[]{:S(2)}, u32[]{:S(2)}) async-start(bf16[16,32,3584]{2,1,0:T(8,128)(2,1)} %bitcast.60), calls=%async_computation.5 | async-start | bytes 7340032 | tf_op jit(solution)/shard_map/all_to_all | solution.py:60
  105.1 55.5 %reduce-scatter.7.cloned.1.call-done = bf16[128,7168]{1,0:T(8,128)(2,1)} async-done(((bf16[512,7168]{1,0:T(8,128)(2,1)}), bf16[128,7168]{1,0:T(8,128)(2,1)}) %reduce-scatter.7.cloned.1.call-update) | async-done | bytes 1835024
  161.0 6.8 %all-to-all-done.5 = bf16[16,32,3584]{2,1,0:T(8,128)(2,1)} async-done(((bf16[16,32,3584]{2,1,0:T(8,128)(2,1)}), bf16[16,32,3584]{2,1,0:T(8,128)(2,1)}, u32[]{:S(2)}, u32[]{:S(2)}) %all-to-all-start.5) | async-done | bytes 3670048 | tf_op jit(solution)/shard_map/all_to_all | solution.py:60
  167.8 2.6 convert_reduce_fusion
  170.4 24.2 %reduce-scatter.9.cloned.1.call-done = bf16[32,7168]{1,0:T(8,128)(2,1)} async-done(((bf16[128,7168]{1,0:T(8,128)(2,1)}), bf16[32,7168]{1,0:T(8,128)(2,1)}) %reduce-scatter.9.cloned.1.call-update) | async-done | bytes 458768 | tf_op jit(solution)/shard_map/reduce_scatter | solution.py:49
  194.6 1.1 convert_element_type.124
  195.7 1.0 multiply_reduce_fusion.3
  197.0 0.7 broadcast_in_dim.25
  197.8 5.0 %all-to-all-start.8 = ((bf16[16,512,16]{1,2,0:T(8,128)(2,1)}), bf16[16,512,16]{1,2,0:T(8,128)(2,1)S(1)}, u32[]{:S(2)}, u32[]{:S(2)}) async-start(bf16[16,512,16]{1,2,0:T(8,128)(2,1)} %broadcast_in_dim.25), calls=%async_computation.8 | async-start | bytes 524288 | tf_op jit(solution)/shard_map/all_to_all | solution.py:13
  203.0 7.2 %all-to-all-done.8 = bf16[16,512,16]{1,2,0:T(8,128)(2,1)S(1)} async-done(((bf16[16,512,16]{1,2,0:T(8,128)(2,1)}), bf16[16,512,16]{1,2,0:T(8,128)(2,1)S(1)}, u32[]{:S(2)}, u32[]{:S(2)}) %all-to-all-start.8) | async-done | bytes 262176 | tf_op jit(solution)/shard_map/all_to_all | solution.py:13
  210.3 0.7 broadcast_in_dim.27
  211.0 3.5 all-to-all-start.10
  214.6 7.5 %all-to-all-done.10 = bf16[16,512,16]{1,2,0:T(8,128)(2,1)S(1)} async-done(((bf16[16,512,16]{1,2,0:T(8,128)(2,1)}), bf16[16,512,16]{1,2,0:T(8,128)(2,1)S(1)}, u32[]{:S(2)}, u32[]{:S(2)}) %all-to-all-start.10) | async-done | bytes 262176 | tf_op jit(solution)/shard_map/all_to_all | solution.py:13
  222.2 0.9 convolution_convert_fusion.4
  223.1 0.9 convolution_convert_fusion.3
  224.1 0.8 pad_maximum_fusion.1
  225.2 12.9 %all_to_all.70 = bf16[16,512,16]{1,2,0:T(8,128)(2,1)S(1)} all-to-all(bf16[16,512,16]{1,2,0:T(8,128)(2,1)S(1)} %broadcast_in_dim.29), channel_id=1, replica_groups=mesh['dp'=8,'mp_0'=4,'mp_1'=4] {'mp_0','mp_1'}, dimensions={0} | all-to-all | bytes 524288 | tf_op jit(solution)/shard_map/all_to_all | solution.py:13
  238.7 0.6 broadcast_in_dim.26
  239.4 8.5 %all-to-all-start.9 = ((f32[8,1,1024]{2,1,0:T(1,128)}), f32[8,1,1024]{2,1,0:T(1,128)S(1)}, u32[]{:S(2)}, u32[]{:S(2)}) async-start(f32[8,1,1024]{2,1,0:T(1,128)} %broadcast_in_dim.26), calls=%async_computation.9 | async-start | bytes 65536 | tf_op jit(solution)/shard_map/all_to_all | solution.py:13
  247.8 30.5 %psum.37 = bf16[3584]{0:T(1024)(128)(2,1)S(1)} all-reduce(bf16[3584]{0:T(1024)(128)(2,1)S(1)} %get-tuple-element.11), channel_id=1, replica_groups=mesh['dp'=8,'mp_0'=4,'mp_1'=4] {'mp_0','mp_1'}, use_global_device_ids=true, to_apply=%region_14.0 | all-reduce | flops 3584 | bytes 14336 | tf_op jit(solution)/shard_map/psum | solution.py:248
  278.4 6.4 %psum.35 = bf16[3584]{0:T(1024)(128)(2,1)S(1)} all-reduce(bf16[3584]{0:T(1024)(128)(2,1)S(1)} %get-tuple-element.12), channel_id=1, replica_groups=mesh['dp'=8,'mp_0'=4,'mp_1'=4] {'mp_0'}, use_global_device_ids=true, to_apply=%region_11.0 | all-reduce | flops 3584 | bytes 14336 | tf_op jit(solution)/shard_map/psum | solution.py:238
  284.8 7.5 %psum.36 = bf16[3584]{0:T(1024)(128)(2,1)S(1)} all-reduce(bf16[3584]{0:T(1024)(128)(2,1)S(1)} %psum.35), channel_id=1, replica_groups=mesh['dp'=8,'mp_0'=4,'mp_1'=4] {'mp_1'}, use_global_device_ids=true, to_apply=%region_12.0 | all-reduce | flops 3584 | bytes 14336 | tf_op jit(solution)/shard_map/psum | solution.py:238
  293.3 17.7 %all_gather.11 = bf16[512,32]{1,0:T(8,128)(2,1)S(1)} all-gather(bf16[32,32]{1,0:T(8,128)(2,1)S(1)} %pad_maximum_fusion.3), channel_id=1, replica_groups=mesh['dp'=8,'mp_0'=4,'mp_1'=4] {'mp_0','mp_1'}, dimensions={0}, use_global_device_ids=true | all-gather | bytes 34816 | tf_op jit(solution)/shard_map/all_gather | solution.py:67
  310.9 0.9 convolution_bitcast_fusion
  311.8 3.1 convolution_convert_fusion.5
  314.9 0.7 broadcast_in_dim.28
  315.6 19.0 %all-to-all-start.11 = ((bf16[8,512,16]{1,2,0:T(8,128)(2,1)}), bf16[8,512,16]{1,2,0:T(8,128)(2,1)S(1)}, u32[]{:S(2)}, u32[]{:S(2)}) async-start(bf16[8,512,16]{1,2,0:T(8,128)(2,1)} %broadcast_in_dim.28), calls=%async_computation.11 | async-start | bytes 262144 | tf_op jit(solution)/shard_map/all_to_all | solution.py:13
  334.6 6.0 %fusion.23 = bf16[512,512]{1,0:T(8,128)(2,1)} fusion(bf16[512,3584]{1,0:T(8,128)(2,1)} %all-gather.3.cloned.1.call-done, bf16[3584,512]{1,0:T(8,128)(2,1)} %get-tuple-element.27), kind=kOutput, calls=%fused_computation.28 | convolution fusion | flops 1879310336 | bytes 7864320 | tf_op jit(solution)/shard_map/dot_general | solution.py:72
  340.6 4.8 %all-to-all-start.2 = ((bf16[8,64,512]{2,1,0:T(8,128)(2,1)}), bf16[8,64,512]{2,1,0:T(8,128)(2,1)S(1)}, u32[]{:S(2)}, u32[]{:S(2)}) async-start(bf16[8,64,512]{2,1,0:T(8,128)(2,1)} %bitcast.3), calls=%async_computation.2 | async-start | bytes 1048576 | tf_op jit(solution)/shard_map/all_to_all | solution.py:60
  345.4 0.8 convolution_bitcast_fusion.1
  346.3 1.6 convert_element_type.146
  347.9 1.6 convert_element_type.151
  349.5 3.5 fusion.45
  352.9 2.0 all-to-all-done.2
  355.0 0.7 fusion.28
  356.2 0.7 reduce.9
  357.5 4.1 all-to-all-start.7
  361.6 43.5 %all-gather.5.cloned.1.call-done = bf16[512,7168]{1,0:T(8,128)(2,1)} async-done(((bf16[32,7168]{1,0:T(8,128)(2,1)}), bf16[512,7168]{1,0:T(8,128)(2,1)}) %all-gather.5.cloned.1.call-update) | async-done | bytes 7340048 | tf_op jit(solution)/shard_map/all_gather | solution.py:67
  405.1 5.4 %fusion.2 = f32[512,512]{1,0:T(8,128)S(1)} fusion(bf16[512,7168]{1,0:T(8,128)(2,1)} %all-gather.5.cloned.1.call-done, bf16[512,3584]{1,0:T(8,128)(2,1)} %get-tuple-element.29), kind=kOutput, calls=%fused_computation.15 | convolution fusion | flops 1879048192 | bytes 8388608 | tf_op jit(solution)/shard_map/dot_general | solution.py:76
  410.5 0.9 copy-done.12
  411.4 2.9 fusion.18
  414.2 4.9 %all-to-all-start.6 = ((bf16[8,64,512]{2,1,0:T(8,128)(2,1)}), bf16[8,64,512]{2,1,0:T(8,128)(2,1)S(1)}, u32[]{:S(2)}, u32[]{:S(2)}) async-start(bf16[8,64,512]{2,1,0:T(8,128)(2,1)} %bitcast.6), calls=%async_computation.6 | async-start | bytes 1048576 | tf_op jit(solution)/shard_map/all_to_all | solution.py:60
  419.2 0.8 fusion.44
  420.6 8.1 %all-to-all-done.6 = bf16[8,64,512]{2,1,0:T(8,128)(2,1)S(1)} async-done(((bf16[8,64,512]{2,1,0:T(8,128)(2,1)}), bf16[8,64,512]{2,1,0:T(8,128)(2,1)S(1)}, u32[]{:S(2)}, u32[]{:S(2)}) %all-to-all-start.6) | async-done | bytes 524320 | tf_op jit(solution)/shard_map/all_to_all | solution.py:60
  428.7 0.7 reduce_sum.175
  (75 shorter events, 5.0 us)
Async XLA Ops:
  7.2 40.8 %copy-start = (bf16[3584,16]{0,1:T(8,128)(2,1)S(1)}, bf16[3584,16]{0,1:T(8,128)(2,1)}, u32[]{:S(2)}) copy-start(bf16[3584,16]{0,1:T(8,128)(2,1)} %param.22) | copy-start | bytes 344068
  8.9 15.3 %all-to-all-start = ((bf16[8,64,512]{2,1,0:T(8,128)(2,1)}), bf16[8,64,512]{2,1,0:T(8,128)(2,1)S(1)}, u32[]{:S(2)}, u32[]{:S(2)}) async-start(bf16[8,64,512]{2,1,0:T(8,128)(2,1)} %broadcast_in_dim.20), calls=%async_computation | async-start | bytes 1048576 | tf_op jit(solution)/shard_map/all_to_all | solution.py:13
  14.7 5.4 %copy-start.3 = (bf16[16,3584]{1,0:T(8,128)(2,1)S(1)}, bf16[16,3584]{1,0:T(8,128)(2,1)}, u32[]{:S(2)}) copy-start(bf16[16,3584]{1,0:T(8,128)(2,1)} %param.21) | copy-start | bytes 344068
  14.7 5.4 %copy-start.5 = (bf16[512,16]{0,1:T(8,128)(2,1)S(1)}, bf16[512,16]{0,1:T(8,128)(2,1)}, u32[]{:S(2)}) copy-start(bf16[512,16]{0,1:T(8,128)(2,1)} %param.20) | copy-start | bytes 49156
  14.7 145.9 %reduce-scatter.7.cloned.1.call-start = ((), (), s32[]{:S(2)}) async-start(), calls=%async_computation.17 | async-start | bytes 9175040
  14.7 5.4 %copy-start.11 = (bf16[512,3584]{1,0:T(8,128)(2,1)S(1)}, bf16[512,3584]{1,0:T(8,128)(2,1)}, u32[]{:S(2)}) copy-start(bf16[512,3584]{1,0:T(8,128)(2,1)} %param.16) | copy-start | bytes 11010052
  24.2 4.3 copy-start.13
  47.9 0.7 copy-start.6
  48.7 13.7 %copy-start.9 = (f32[512]{0:T(512)S(1)}, f32[512]{0:T(512)}, u32[]{:S(2)}) copy-start(f32[512]{0:T(512)} %param.26) | copy-start | bytes 6148
  48.7 13.7 %copy-start.1 = (bf16[64,512]{1,0:T(8,128)(2,1)S(1)}, bf16[64,512]{1,0:T(8,128)(2,1)}, u32[]{:S(2)}) copy-start(bf16[64,512]{1,0:T(8,128)(2,1)} %param.27) | copy-start | bytes 196612
  63.3 13.5 %all-to-all-start.4 = ((bf16[8,64,512]{2,1,0:T(8,128)(2,1)}), bf16[8,64,512]{2,1,0:T(8,128)(2,1)S(1)}, u32[]{:S(2)}, u32[]{:S(2)}) async-start(bf16[8,64,512]{2,1,0:T(8,128)(2,1)} %broadcast_in_dim.23), calls=%async_computation.4 | async-start | bytes 1048576 | tf_op jit(solution)/shard_map/all_to_all | solution.py:13
  77.8 21.2 %all-to-all-start.1 = ((f32[16,1,7168]{2,1,0:T(1,128)}), f32[16,1,7168]{2,1,0:T(1,128)S(1)}, u32[]{:S(2)}, u32[]{:S(2)}) async-start(f32[16,1,7168]{2,1,0:T(1,128)} %broadcast_in_dim.21), calls=%async_computation.1 | async-start | bytes 917504 | tf_op jit(solution)/shard_map/all_to_all | solution.py:13
  99.0 61.9 %copy-start.7 = (f32[3584]{0:T(1024)S(1)}, f32[3584]{0:T(1024)}, u32[]{:S(2)}) copy-start(f32[3584]{0:T(1024)} %param.24) | copy-start | bytes 43012
  99.0 61.9 %copy-start.8 = (f32[3584]{0:T(1024)S(1)}, f32[3584]{0:T(1024)}, u32[]{:S(2)}) copy-start(f32[3584]{0:T(1024)} %param.25) | copy-start | bytes 43012
  99.0 68.8 %all-to-all-start.5 = ((bf16[16,32,3584]{2,1,0:T(8,128)(2,1)}), bf16[16,32,3584]{2,1,0:T(8,128)(2,1)}, u32[]{:S(2)}, u32[]{:S(2)}) async-start(bf16[16,32,3584]{2,1,0:T(8,128)(2,1)} %bitcast.60), calls=%async_computation.5 | async-start | bytes 7340032 | tf_op jit(solution)/shard_map/all_to_all | solution.py:60
  105.0 89.6 %reduce-scatter.9.cloned.1.call-start = ((), (), s32[]{:S(2)}) async-start(), calls=%async_computation.18 | async-start | bytes 2293760 | tf_op jit(solution)/shard_map/reduce_scatter | solution.py:49
  160.6 151.2 %all-gather.3.cloned.1.call-start = ((), (), s32[]{:S(2)}) async-start(), calls=%async_computation.15 | async-start | bytes 3899392 | tf_op jit(solution)/shard_map/all_gather | solution.py:181
  161.0 35.8 %copy-start.4 = (bf16[512,16]{0,1:T(8,128)(2,1)S(1)}, bf16[512,16]{0,1:T(8,128)(2,1)}, u32[]{:S(2)}) copy-start(bf16[512,16]{0,1:T(8,128)(2,1)} %param.18) | copy-start | bytes 49156
  197.0 41.1 %copy-start.2 = (bf16[16,3584]{1,0:T(8,128)(2,1)S(1)}, bf16[16,3584]{1,0:T(8,128)(2,1)}, u32[]{:S(2)}) copy-start(bf16[16,3584]{1,0:T(8,128)(2,1)} %param.19) | copy-start | bytes 344068
  197.8 12.5 %all-to-all-start.8 = ((bf16[16,512,16]{1,2,0:T(8,128)(2,1)}), bf16[16,512,16]{1,2,0:T(8,128)(2,1)S(1)}, u32[]{:S(2)}, u32[]{:S(2)}) async-start(bf16[16,512,16]{1,2,0:T(8,128)(2,1)} %broadcast_in_dim.25), calls=%async_computation.8 | async-start | bytes 524288 | tf_op jit(solution)/shard_map/all_to_all | solution.py:13
  211.0 11.2 %all-to-all-start.10 = ((bf16[16,512,16]{1,2,0:T(8,128)(2,1)}), bf16[16,512,16]{1,2,0:T(8,128)(2,1)S(1)}, u32[]{:S(2)}, u32[]{:S(2)}) async-start(bf16[16,512,16]{1,2,0:T(8,128)(2,1)} %broadcast_in_dim.27), calls=%async_computation.10 | async-start | bytes 524288 | tf_op jit(solution)/shard_map/all_to_all | solution.py:13
  214.5 131.7 %all-reduce.3.cloned.1.call-start = ((), (), s32[]{:S(2)}) async-start(), calls=%async_computation.19 | async-start | bytes 458752 | tf_op jit(solution)/shard_map/psum | solution.py:249
  224.0 181.1 %all-gather.5.cloned.1.call-start = ((), (), s32[]{:S(2)}) async-start(), calls=%async_computation.16 | async-start | bytes 7798784 | tf_op jit(solution)/shard_map/all_gather | solution.py:67
  239.4 53.6 %all-to-all-start.9 = ((f32[8,1,1024]{2,1,0:T(1,128)}), f32[8,1,1024]{2,1,0:T(1,128)S(1)}, u32[]{:S(2)}, u32[]{:S(2)}) async-start(f32[8,1,1024]{2,1,0:T(1,128)} %broadcast_in_dim.26), calls=%async_computation.9 | async-start | bytes 65536 | tf_op jit(solution)/shard_map/all_to_all | solution.py:13
  315.6 25.1 %all-to-all-start.11 = ((bf16[8,512,16]{1,2,0:T(8,128)(2,1)}), bf16[8,512,16]{1,2,0:T(8,128)(2,1)S(1)}, u32[]{:S(2)}, u32[]{:S(2)}) async-start(bf16[8,512,16]{1,2,0:T(8,128)(2,1)} %broadcast_in_dim.28), calls=%async_computation.11 | async-start | bytes 262144 | tf_op jit(solution)/shard_map/all_to_all | solution.py:13
  340.6 14.3 %all-to-all-start.2 = ((bf16[8,64,512]{2,1,0:T(8,128)(2,1)}), bf16[8,64,512]{2,1,0:T(8,128)(2,1)S(1)}, u32[]{:S(2)}, u32[]{:S(2)}) async-start(bf16[8,64,512]{2,1,0:T(8,128)(2,1)} %bitcast.3), calls=%async_computation.2 | async-start | bytes 1048576 | tf_op jit(solution)/shard_map/all_to_all | solution.py:60
  357.5 56.8 %all-to-all-start.7 = ((bf16[8,2,256]{2,1,0:T(2,128)(2,1)}), bf16[8,2,256]{2,1,0:T(2,128)(2,1)S(1)}, u32[]{:S(2)}, u32[]{:S(2)}) async-start(bf16[8,2,256]{2,1,0:T(2,128)(2,1)} %reshape.111), calls=%async_computation.7 | async-start | bytes 16384 | tf_op jit(solution)/shard_map/all_to_all | solution.py:13
  405.1 5.4 %copy-start.10 = (bf16[512,7168]{1,0:T(8,128)(2,1)S(1)}, bf16[512,7168]{1,0:T(8,128)(2,1)}, u32[]{:S(2)}) copy-start(bf16[512,7168]{1,0:T(8,128)(2,1)} %all-gather.5.cloned.1.call-done) | copy-start | bytes 22020100
  405.1 6.3 %copy-start.12 = (bf16[512,3584]{1,0:T(8,128)(2,1)S(1)}, bf16[512,3584]{1,0:T(8,128)(2,1)}, u32[]{:S(2)}) copy-start(bf16[512,3584]{1,0:T(8,128)(2,1)} %get-tuple-element.31) | copy-start | bytes 11010052
  414.2 14.4 %all-to-all-start.6 = ((bf16[8,64,512]{2,1,0:T(8,128)(2,1)}), bf16[8,64,512]{2,1,0:T(8,128)(2,1)S(1)}, u32[]{:S(2)}, u32[]{:S(2)}) async-start(bf16[8,64,512]{2,1,0:T(8,128)(2,1)} %bitcast.6), calls=%async_computation.6 | async-start | bytes 1048576 | tf_op jit(solution)/shard_map/all_to_all | solution.py:60
Sparse Core Ops, SparseCore 0:
  48.1 112.4 reduce-scatter.6
  163.0 31.6 reduce-scatter.8
  197.4 52.6 all-gather.2
  253.9 82.0 all-reduce.2
  338.3 66.7 all-gather.4
